TPU v7x, 32 devices: a whole 2x2x4 slice. The times are simulated.
32 devices in a mesh: row: 4 (over z), col: 4 (over y, core), rep: 2 (over x).
Axes of the slice: x: 2, y: 2, z: 4, core: 2. Of those that a mesh axis runs over, the one named last changes fastest.
Arguments:
- spectra: bfloat16 [2, 8, 64, 2048], P(None, 'row', 'rep', 'col'), parts along dimension 2, may hold values from -60 to 60, as said below
Outputs:
- correlation: bfloat16 [12, 2048, 2048], P('rep', 'row', 'col'), parts along dimension 0
There are 2 independent parts, one for each index of `rep`. A program takes and returns all parts, laid end to end along the dimension named above; each array names one. Nothing has to cross between parts.
Inputs may be any that keep to these rules, and one draw needn't show every extreme that they name: `spectra`: spectral samples.
All inputs are finite; a program needn't handle non-finite values.
Results may differ from a plain program's by a relative error of at most 0.0065.
Values may be sent and summed in bfloat16 or wider, within the bound.
A program may use at most 64 MiB of HBM per device.

v0:
```python
import math

import jax
import jax.numpy as jnp
from jax import lax
from jax.sharding import PartitionSpec as P

LAGS = 6


def whiten(spectra):
    values = spectra.astype(jnp.float32)
    power = jnp.mean(values * values, axis=(0, 2), keepdims=True)
    return (values / jnp.sqrt(power + 1e-05)).astype(jnp.bfloat16)


def phase_tables(bins, lags):
    freq = jnp.arange(bins).astype(jnp.float32) + 1.0
    shift = 2.0 * jnp.arange(lags).astype(jnp.float32) - lags + 1.0
    angle = math.pi * shift[:, None] * freq[None, :] / bins
    return (jnp.cos(angle), jnp.sin(angle))


def rotate(side, cosine, sine):
    values = side.astype(jnp.float32)
    c_term = cosine[:, None, :, None]
    s_term = sine[:, None, :, None]
    real_part = values[0][None] * c_term - values[1][None] * s_term
    imag_part = values[0][None] * s_term + values[1][None] * c_term
    return jnp.stack([real_part, imag_part], axis=1).astype(jnp.bfloat16)


def correlate(row_side, turned):
    return jnp.einsum("kwfi,tkwfj->tij", row_side, turned, preferred_element_type=jnp.float32)


def body(spectra):
    white = whiten(spectra)
    col_side = lax.all_gather(white, "row", axis=1, tiled=True)
    bins = spectra.shape[2]
    cosine, sine = phase_tables(bins, LAGS)
    turned = rotate(col_side, cosine, sine)
    scale = 1.0 / math.sqrt(col_side.shape[1] * bins)
    local_all = lax.all_gather(white, "col", axis=3, tiled=True)
    row_side = lax.all_to_all(local_all, "row", split_axis=3, concat_axis=1, tiled=True)
    total = correlate(row_side, turned)
    return (total * scale).astype(jnp.bfloat16)


def solution(mesh):
    in_specs = (P(None, "row", "rep", "col"),)
    out_specs = P("rep", "row", "col")
    return jax.shard_map(body, mesh=mesh, in_specs=in_specs, out_specs=out_specs, check_vma=False)
```

profile of v0, /device:TPU:0, one launch (start us, length us, event | category | flops | bytes accessed | tf_op | source)
XLA Modules:
  0.0 59.6 jit_solution(18240609285780552811)
XLA Ops:
  0.0 0.9 %fusion.8 = f32[2,512]{1,0:T(2,128)S(1)} fusion(bf16[2,2,32,512]{3,2,1,0:T(8,128)(2,1)} %param.1), kind=kLoop, calls=%fused_computation.13 | loop fusion | flops 195584 | bytes 135168 | tf_op jit(solution)/shard_map/reduce_sum | solution.py:13
  1.0 0.9 %fusion.9 = bf16[2,2,32,512]{3,2,0,1:T(8,128)(2,1)S(1)} fusion(f32[2,512]{1,0:T(2,128)S(1)} %add_sqrt_fusion, bf16[2,2,32,512]{3,2,1,0:T(8,128)(2,1)} %param.1), kind=kLoop, calls=%fused_computation.14 | loop fusion | flops 196608 | bytes 266240 | tf_op jit(solution)/shard_map/convert_element_type | solution.py:14
  1.9 8.6 %all_gather.7 = bf16[2,2,32,2048]{3,2,1,0:T(8,128)(2,1)S(1)} all-gather(bf16[2,2,32,512]{3,2,1,0:T(8,128)(2,1)S(1)} %copy.10), channel_id=1, replica_groups=mesh['row'=4,'col'=4,'rep'=2] {'col'}, dimensions={3}, use_global_device_ids=true | all-gather | bytes 655360 | tf_op jit(solution)/shard_map/all_gather | solution.py:44
  10.6 1.5 %copy.11 = bf16[2,2,32,2048]{2,1,0,3:T(2,128)(2,1)S(1)} copy(bf16[2,2,32,2048]{3,2,1,0:T(8,128)(2,1)S(1)} %all_gather.7) | data formatting | bytes 1048576 | tf_op jit(solution)/shard_map/all_gather | solution.py:44
  12.1 2.9 %reshape.95 = bf16[4,2,32768]{2,1,0:T(2,128)(2,1)} reshape(bf16[2048,2,2,32]{3,2,1,0:T(2,128)(2,1)S(1)} %bitcast.25) | data formatting | bytes 1048576
  15.0 4.9 %all-to-all-start = ((bf16[4,2,32768]{2,1,0:T(2,128)(2,1)}), bf16[4,2,32768]{2,1,0:T(2,128)(2,1)S(1)}, u32[]{:S(2)}, u32[]{:S(2)}) async-start(bf16[4,2,32768]{2,1,0:T(2,128)(2,1)} %reshape.95), calls=%async_computation | async-start | bytes 1048576 | tf_op jit(solution)/shard_map/all_to_all | solution.py:45
  19.9 24.8 %all_gather.6 = bf16[2,8,32,512]{3,2,0,1:T(8,128)(2,1)S(1)} all-gather(bf16[2,2,32,512]{3,2,0,1:T(8,128)(2,1)S(1)} %fusion.9), channel_id=1, replica_groups=mesh['row'=4,'col'=4,'rep'=2] {'row'}, dimensions={1}, use_global_device_ids=true | all-gather | bytes 655360 | tf_op jit(solution)/shard_map/all_gather | solution.py:39
  44.7 0.1 convert_element_type.44
  44.8 0.1 fusion.11
  44.9 0.1 slice_bitcast_fusion.1
  45.0 2.7 %subtract_convert_fusion = (bf16[6,1,8,32,512]{4,3,2,0,1:T(8,128)(2,1)}, bf16[6,1,8,32,512]{4,3,2,0,1:T(8,128)(2,1)}) fusion(f32[6,32]{1,0:T(8,128)S(1)} %get-tuple-element.10, f32[8,32,512]{2,1,0:T(8,128)S(1)} %get-tuple-element.8, f32[6,32]{1,0:T(8,128)S(1)} %get-tuple-element.9, f32[8,32,512]{2,1,0:T(8,128)S(1)} %get-tuple-element.7), kind=kLoop, calls=%fused_computation.8 | loop fusion | flops 6291456 | bytes 4195840 | tf_op jit(solution)/shard_map/convert
  47.8 0.0 all-to-all-done
  47.8 1.1 %reshape.96 = bf16[2048,2,2,32]{3,2,1,0:T(2,128)(2,1)S(1)} reshape(bf16[4,2,32768]{2,1,0:T(2,128)(2,1)S(1)} %all-to-all-done) | data formatting | bytes 1048576
  48.9 4.2 %copy.12 = bf16[2,2,32,4,512]{4,2,1,3,0:T(8,128)(2,1)} copy(bf16[2,2,32,4,512]{2,1,0,4,3:T(2,128)(2,1)S(1)} %bitcast.26) | data formatting | bytes 1048576 | tf_op jit(solution)/shard_map/all_to_all | solution.py:45
  53.0 3.8 %fusion.1 = bf16[6,512,512]{1,2,0:T(8,128)(2,1)S(1)} fusion(bf16[2,8,32,512,1]{3,2,1,4,0:T(8,128)(2,1)} %bitcast.27, bf16[6,1,8,32,512]{4,3,2,0,1:T(8,128)(2,1)} %get-tuple-element.6, bf16[6,1,8,32,512]{4,3,2,0,1:T(8,128)(2,1)} %get-tuple-element.5), kind=kOutput, calls=%fused_computation.2 | convolution fusion | flops 1615331328 | bytes 6815744 | tf_op jit(solution)/shard_map/kwfi,tkwfj->tij/dot_general | solution.py:34
  56.9 2.8 %copy.13 = bf16[6,512,512]{2,1,0:T(8,128)(2,1)} copy(bf16[6,512,512]{1,2,0:T(8,128)(2,1)S(1)} %fusion.1) | data formatting | bytes 6291456 | tf_op jit(solution)/shard_map/convert_element_type | solution.py:47
  (4 shorter events, 0.0 us)
Async XLA Ops:
  15.0 32.8 %all-to-all-start = ((bf16[4,2,32768]{2,1,0:T(2,128)(2,1)}), bf16[4,2,32768]{2,1,0:T(2,128)(2,1)S(1)}, u32[]{:S(2)}, u32[]{:S(2)}) async-start(bf16[4,2,32768]{2,1,0:T(2,128)(2,1)} %reshape.95), calls=%async_computation | async-start | bytes 1048576 | tf_op jit(solution)/shard_map/all_to_all | solution.py:45
where the time goes:
time: 59.9 us; the launch traced here: 59.6 us
  blocking collectives  33.5 us (56%)
  local copies, waits for them, and re-layouts  12.5 us (21%)
  starting transfers between devices  4.87 us (8%)
  other arithmetic  4.86 us (8%)
  matrix products  3.84 us (6%)
    all_gather x1, blocking collectives, body(): col_side = lax.all_gather(white, 'row', axis=1, tiled=True)  24.8 us
    all_gather x1, blocking collectives, body(): local_all = lax.all_gather(white, 'col', axis=3, tiled=True)  8.65 us
    all_to_all x1, starting transfers between devices, body(): lax.all_to_all(local_all, 'row', split_axis=3, concat_axis=1, tiled=True)  4.87 us
    all_to_all x1, local copies, waits for them, and re-layouts, body(): lax.all_to_all(local_all, 'row', split_axis=3, concat_axis=1, tiled=True)  4.15 us
    unnamed x2, local copies, waits for them, and re-layouts  4 us
    dot_general x1, matrix products, correlate(): jnp.einsum('kwfi,tkwfj->tij', row_side, turned, preferred_element_type=jn...  3.84 us
    convert_element_type x1, local copies, waits for them, and re-layouts, body(): return (total * scale).astype(jnp.bfloat16)  2.78 us
    another operation x1, other arithmetic  2.73 us
  transfers between devices with their start and end apart: 1, of which 0 were waited for; matrix products, arithmetic and copies ran while one was open for 5% of the time, Pallas kernels for 0%

commit v1 on v0

v1 whole, which is shorter than its diff:
```python
import functools
import math

import jax
import jax.numpy as jnp
import numpy as np
from jax import lax
from jax.experimental import pallas as pl
from jax.experimental.pallas import tpu as pltpu
from jax.sharding import PartitionSpec as P

LAGS = 6
MESH = pl.DeviceIdType.MESH
LEFT, RIGHT = 0, 1


def phase_table(bins, lags):
    freq = np.arange(bins, dtype=np.float32) + np.float32(1.0)
    shift = np.float32(2.0) * np.arange(lags, dtype=np.float32) - np.float32(lags - 1.0)
    angle = (np.float32(math.pi) * shift[None, :] * freq[:, None] / np.float32(bins)).astype(np.float32)
    return np.concatenate([np.cos(angle), np.sin(angle)], axis=1).astype(np.float32)


def kernel(n, m, scale, x_hbm, tab_hbm, out_ref, x, tab, col, row, row_t, turned,
           in_sem, z_send, z_recv, c_send, f_send, r_recv):
    _, wl, bins, cl = x.shape
    half = wl * bins
    depth = 2 * half
    q = m // n
    chips = m // 2
    r = lax.axis_index("row")
    c = lax.axis_index("col")
    chip = c // 2
    core = c % 2
    sib = chip * 2 + (1 - core)

    load_x = pltpu.make_async_copy(x_hbm, x, in_sem.at[0])
    load_t = pltpu.make_async_copy(tab_hbm, tab, in_sem.at[1])
    load_x.start()
    load_t.start()

    barrier = pltpu.get_barrier_semaphore()
    for d in range(1, m):
        pl.semaphore_signal(barrier, inc=1, device_id={"col": (c + d) % m}, device_id_type=MESH)

    @pl.when(r > 0)
    def _():
        pl.semaphore_signal(barrier, inc=1, device_id={"row": r - 1}, device_id_type=MESH)

    @pl.when(r < n - 1)
    def _():
        pl.semaphore_signal(barrier, inc=1, device_id={"row": r + 1}, device_id_type=MESH)

    load_x.wait()
    for w in range(wl):
        re = x[0, w].astype(jnp.float32)
        im = x[1, w].astype(jnp.float32)
        power = jnp.sum(re * re + im * im, axis=0, keepdims=True) / (2.0 * bins)
        root = jnp.sqrt(power + 1e-05)
        col[r, 0, w * bins:(w + 1) * bins, :] = (re / root).astype(jnp.bfloat16)
        col[r, 1, w * bins:(w + 1) * bins, :] = (im / root).astype(jnp.bfloat16)

    pl.semaphore_wait(barrier, (m - 1) + (r > 0).astype(jnp.int32) + (r < n - 1).astype(jnp.int32))

    def z_copy(way, s, part):
        src = r - s if way == RIGHT else r + s
        to = r + 1 if way == RIGHT else r - 1
        return pltpu.make_async_remote_copy(
            src_ref=col.at[src, part], dst_ref=col.at[src, part],
            send_sem=z_send.at[way, s, part], recv_sem=z_recv.at[way, s, part],
            device_id={"row": to}, device_id_type=MESH)

    def z_sends(way, s):
        if way == RIGHT:
            return jnp.logical_and(r - s >= 0, r + 1 < n)
        return jnp.logical_and(r + s < n, r - 1 >= 0)

    def z_got(way, s):
        if way == RIGHT:
            return r - 1 - s >= 0
        return r + 1 + s < n

    def z_src(way, s):
        return r - 1 - s if way == RIGHT else r + 1 + s

    def slot_of(way, s):
        return 1 + 2 * s + way

    def owns(o):
        return c == r * q + o

    def own_copies(o, src, slot, part):
        copies = []
        for p in range(1, chips):
            copies.append(pltpu.make_async_remote_copy(
                src_ref=col.at[src, part], dst_ref=row.at[o, src, part],
                send_sem=c_send.at[slot, part, p], recv_sem=r_recv.at[o, slot, part],
                device_id={"col": ((chip + p) % chips) * 2 + part}, device_id_type=MESH))
        copies.append(pltpu.make_async_remote_copy(
            src_ref=col.at[src, part], dst_ref=row.at[o, src, part],
            send_sem=c_send.at[slot, part, 0], recv_sem=r_recv.at[o, slot, part],
            device_id={"col": sib}, device_id_type=MESH))
        return copies

    def swap_copy(o, src, slot, part):
        return pltpu.make_async_remote_copy(
            src_ref=row.at[o, src, part], dst_ref=row.at[o, src, part],
            send_sem=f_send.at[o, slot], recv_sem=r_recv.at[o, slot, part],
            device_id={"col": sib}, device_id_type=MESH)

    def hand_out(src, slot, part):
        for o in range(q):
            @pl.when(owns(o))
            def _():
                for copy in own_copies(o, src, slot, part):
                    copy.start()

    def far(o):
        return chip != (r * q + o) // 2

    def swap(src, slot):
        for o in range(q):
            for part in range(2):
                @pl.when(jnp.logical_and(far(o), core == part))
                def _():
                    swap_copy(o, src, slot, part).wait_recv()
                    swap_copy(o, src, slot, part).start()

    def turn(src):
        base = pl.multiple_of(src * depth, depth)
        for w in range(wl):
            rows = slice(w * bins, (w + 1) * bins)
            re = col[src, 0, rows, :].astype(jnp.float32)
            im = col[src, 1, rows, :].astype(jnp.float32)
            for t in range(LAGS):
                cos = tab[:, t:t + 1]
                sin = tab[:, LAGS + t:LAGS + t + 1]
                turned[t, pl.ds(base + w * bins, bins), :] = (re * cos - im * sin).astype(jnp.bfloat16)
                turned[t, pl.ds(base + half + w * bins, bins), :] = (re * sin + im * cos).astype(jnp.bfloat16)

    def flip(src, slot):
        base = pl.multiple_of(src * depth, depth)
        for o in range(q):
            chans = slice(o * cl, (o + 1) * cl)

            @pl.when(owns(o))
            def _():
                row_t[chans, pl.ds(base, depth)] = col[src].reshape(depth, cl).T

            @pl.when(jnp.logical_not(owns(o)))
            def _():
                for part in range(2):
                    @pl.when(jnp.logical_or(jnp.logical_not(far(o)), core != part))
                    def _():
                        swap_copy(o, src, slot, part).wait_recv()
                row_t[chans, pl.ds(base, depth)] = row[o, src].reshape(depth, cl).T

    for part in range(2):
        for way in (LEFT, RIGHT):
            @pl.when(z_sends(way, 0))
            def _():
                z_copy(way, 0, part).start()
        hand_out(r, 0, part)
    load_t.wait()
    turn(r)

    def each(s, fn):
        if s < 0:
            fn(r, 0)
            return
        for way in (LEFT, RIGHT):
            @pl.when(z_got(way, s))
            def _():
                fn(z_src(way, s), slot_of(way, s))

    for s in range(n - 1):
        for part in range(2):
            for way in (LEFT, RIGHT):
                @pl.when(z_got(way, s))
                def _():
                    z_copy(way, s, part).wait_recv()
                    if s + 1 < n - 1:
                        @pl.when(z_sends(way, s + 1))
                        def _():
                            z_copy(way, s + 1, part).start()
                    hand_out(z_src(way, s), slot_of(way, s), part)
        each(s - 1, swap)
        each(s, lambda src, slot: turn(src))
        each(s - 1, flip)
    each(n - 2, swap)
    each(n - 2, flip)

    for t in range(LAGS):
        total = jnp.dot(row_t[...], turned[t], preferred_element_type=jnp.float32)
        out_ref[t] = (total * scale).astype(out_ref.dtype)

    for s in range(n - 1):
        for way in (LEFT, RIGHT):
            @pl.when(z_sends(way, s))
            def _():
                for part in range(2):
                    z_copy(way, s, part).wait_send()

    def drain(src, slot):
        for o in range(q):
            @pl.when(owns(o))
            def _():
                for part in range(2):
                    for copy in own_copies(o, src, slot, part):
                        copy.wait_send()
            for part in range(2):
                @pl.when(jnp.logical_and(far(o), core == part))
                def _():
                    swap_copy(o, src, slot, part).wait_send()

    for s in range(-1, n - 1):
        each(s, drain)


def correlate(n, m, spectra):
    _, wl, bins, cl = spectra.shape
    q = m // n
    half = wl * bins
    depth = 2 * half
    slots = 2 * n - 1
    scale = 1.0 / math.sqrt(n * wl * bins)
    table = jnp.asarray(phase_table(bins, LAGS))
    sizes = (n * depth * cl * (1 + 2 * q + LAGS) + LAGS * q * cl * cl) * 2
    dma = pltpu.SemaphoreType.DMA
    return pl.pallas_call(
        functools.partial(kernel, n, m, scale),
        out_shape=pltpu.VMEM((LAGS, q * cl, cl), jnp.bfloat16),
        in_specs=[pl.BlockSpec(memory_space=pltpu.HBM)] * 2,
        out_specs=pl.BlockSpec(memory_space=pltpu.VMEM),
        scratch_shapes=[
            pltpu.VMEM(spectra.shape, jnp.bfloat16),
            pltpu.VMEM(table.shape, jnp.float32),
            pltpu.VMEM((n, 2, half, cl), jnp.bfloat16),
            pltpu.VMEM((q, n, 2, half, cl), jnp.bfloat16),
            pltpu.VMEM((q * cl, n * depth), jnp.bfloat16),
            pltpu.VMEM((LAGS, n * depth, cl), jnp.bfloat16),
            dma((2,)),
            dma((2, n - 1, 2)),
            dma((2, n - 1, 2)),
            dma((slots, 2, m // 2)),
            dma((q, slots)),
            dma((q, slots, 2)),
        ],
        compiler_params=pltpu.CompilerParams(
            collective_id=0, has_side_effects=True, vmem_limit_bytes=sizes + (16 << 20)),
        cost_estimate=pl.CostEstimate(
            flops=2 * LAGS * n * depth * q * cl * cl,
            bytes_accessed=LAGS * q * cl * cl * 2, transcendentals=0),
    )(spectra, table)


def solution(mesh):
    n, m = mesh.shape["row"], mesh.shape["col"]
    return jax.shard_map(
        functools.partial(correlate, n, m), mesh=mesh,
        in_specs=(P(None, "row", "rep", "col"),), out_specs=P("rep", "row", "col"), check_vma=False)
```

time: 59.9 us -> 24.7 us (0.41)
  the two profiles are of different devices: /device:TPU:0 before, /device:TPU:5 now
where the time goes in v1:
time: 24.7 us; the launch traced here: 24.5 us
  Pallas kernels  21.2 us (86%)
  local copies, waits for them, and re-layouts  3.29 us (13%)
    pallas_call x1, Pallas kernels, correlate(): pl.pallas_call(functools.partial(kernel, n, m, scale), out_shape=pltpu.VM...  21.2 us
    unnamed x5, local copies, waits for them, and re-layouts  3.29 us

profile of v1, /device:TPU:5, one launch (start us, length us, event | category | flops | bytes accessed | tf_op | source)
XLA Modules:
  0.0 24.5 jit_solution(10980291454896106868)
XLA Ops:
  0.0 0.0 copy-start
  0.0 0.9 %copy-done = bf16[2,2,32,512]{3,2,1,0:T(8,128)(2,1)S(1)} copy-done((bf16[2,2,32,512]{3,2,1,0:T(8,128)(2,1)S(1)}, bf16[2,2,32,512]{3,2,1,0:T(8,128)(2,1)}, u32[]{:S(2)}) %copy-start) | copy-done | bytes 131096
  0.9 0.0 copy-start.1
  0.9 0.7 %copy-done.1 = f32[32,12]{1,0:T(8,128)S(1)} copy-done((f32[32,12]{1,0:T(8,128)S(1)}, f32[32,12]{1,0:T(8,128)}, u32[]{:S(2)}) %copy-start.1) | copy-done | bytes 1560
  1.6 21.2 %shard_map.28 = bf16[6,512,512]{2,1,0:T(8,128)(2,1)S(1)} custom-call(bf16[2,2,32,512]{3,2,1,0:T(8,128)(2,1)S(1)} %copy-done, f32[32,12]{1,0:T(8,128)S(1)} %copy-done.1), custom_call_target="tpu_custom_call" | custom-call | flops 1610612736 | bytes 3145728 | tf_op jit(solution)/shard_map/pallas_call | solution.py:230
  22.8 1.7 %copy.4 = bf16[6,512,512]{2,1,0:T(8,128)(2,1)} copy(bf16[6,512,512]{2,1,0:T(8,128)(2,1)S(1)} %shard_map.28) | data formatting | bytes 6291456
Async XLA Ops:
  0.0 0.9 %copy-start = (bf16[2,2,32,512]{3,2,1,0:T(8,128)(2,1)S(1)}, bf16[2,2,32,512]{3,2,1,0:T(8,128)(2,1)}, u32[]{:S(2)}) copy-start(bf16[2,2,32,512]{3,2,1,0:T(8,128)(2,1)} %x_hbm.1) | copy-start | bytes 393220
  0.9 0.7 %copy-start.1 = (f32[32,12]{1,0:T(8,128)S(1)}, f32[32,12]{1,0:T(8,128)}, u32[]{:S(2)}) copy-start(f32[32,12]{1,0:T(8,128)} %constant.2.clone.tab_hbm) | copy-start | bytes 4612

commit v2 on v1

--- a/solution.py
+++ b/solution.py
@@ -21,7 +21,7 @@
     return np.concatenate([np.cos(angle), np.sin(angle)], axis=1).astype(np.float32)
 
 
-def kernel(n, m, scale, x_hbm, tab_hbm, out_ref, x, tab, col, row, row_t, turned,
+def gather(n, m, x_hbm, tab_hbm, row_t, turned, x, tab, col, row,
            in_sem, z_send, z_recv, c_send, f_send, r_recv):
     _, wl, bins, cl = x.shape
     half = wl * bins
@@ -190,10 +190,6 @@
     each(n - 2, swap)
     each(n - 2, flip)
 
-    for t in range(LAGS):
-        total = jnp.dot(row_t[...], turned[t], preferred_element_type=jnp.float32)
-        out_ref[t] = (total * scale).astype(out_ref.dtype)
-
     for s in range(n - 1):
         for way in (LEFT, RIGHT):
             @pl.when(z_sends(way, s))
@@ -217,6 +213,17 @@
         each(s, drain)
 
 
+def multiply(scale, row_t, turned, out_hbm, out, sem):
+    copies = []
+    for t in range(LAGS):
+        total = jnp.dot(row_t[...], turned[t], preferred_element_type=jnp.float32)
+        out[t] = (total * scale).astype(out.dtype)
+        copies.append(pltpu.make_async_copy(out.at[t], out_hbm.at[t], sem.at[t]))
+        copies[t].start()
+    for copy in copies:
+        copy.wait()
+
+
 def correlate(n, m, spectra):
     _, wl, bins, cl = spectra.shape
     q = m // n
@@ -224,21 +231,22 @@
     depth = 2 * half
     slots = 2 * n - 1
     scale = 1.0 / math.sqrt(n * wl * bins)
-    table = jnp.asarray(phase_table(bins, LAGS))
-    sizes = (n * depth * cl * (1 + 2 * q + LAGS) + LAGS * q * cl * cl) * 2
+    spectra = pltpu.with_memory_space_constraint(spectra, pltpu.HBM)
+    table = pltpu.with_memory_space_constraint(jnp.asarray(phase_table(bins, LAGS)), pltpu.HBM)
     dma = pltpu.SemaphoreType.DMA
-    return pl.pallas_call(
-        functools.partial(kernel, n, m, scale),
-        out_shape=pltpu.VMEM((LAGS, q * cl, cl), jnp.bfloat16),
-        in_specs=[pl.BlockSpec(memory_space=pltpu.HBM)] * 2,
-        out_specs=pl.BlockSpec(memory_space=pltpu.VMEM),
+    vmem = pl.BlockSpec(memory_space=pltpu.VMEM)
+    hbm = pl.BlockSpec(memory_space=pltpu.HBM)
+    row_t, turned = pl.pallas_call(
+        functools.partial(gather, n, m),
+        out_shape=(pltpu.VMEM((q * cl, n * depth), jnp.bfloat16),
+                   pltpu.VMEM((LAGS, n * depth, cl), jnp.bfloat16)),
+        in_specs=[hbm, hbm],
+        out_specs=(vmem, vmem),
         scratch_shapes=[
             pltpu.VMEM(spectra.shape, jnp.bfloat16),
             pltpu.VMEM(table.shape, jnp.float32),
             pltpu.VMEM((n, 2, half, cl), jnp.bfloat16),
             pltpu.VMEM((q, n, 2, half, cl), jnp.bfloat16),
-            pltpu.VMEM((q * cl, n * depth), jnp.bfloat16),
-            pltpu.VMEM((LAGS, n * depth, cl), jnp.bfloat16),
             dma((2,)),
             dma((2, n - 1, 2)),
             dma((2, n - 1, 2)),
@@ -247,11 +255,21 @@
             dma((q, slots, 2)),
         ],
         compiler_params=pltpu.CompilerParams(
-            collective_id=0, has_side_effects=True, vmem_limit_bytes=sizes + (16 << 20)),
-        cost_estimate=pl.CostEstimate(
-            flops=2 * LAGS * n * depth * q * cl * cl,
-            bytes_accessed=LAGS * q * cl * cl * 2, transcendentals=0),
+            collective_id=0, has_side_effects=True,
+            vmem_limit_bytes=2 * n * depth * cl * (2 + q) + (8 << 20)),
+        name="gather",
     )(spectra, table)
+    row_t = pltpu.with_memory_space_constraint(row_t, pltpu.VMEM)
+    turned = pltpu.with_memory_space_constraint(turned, pltpu.VMEM)
+    return pl.pallas_call(
+        functools.partial(multiply, scale),
+        out_shape=jax.ShapeDtypeStruct((LAGS, q * cl, cl), jnp.bfloat16),
+        in_specs=[vmem, vmem],
+        out_specs=hbm,
+        scratch_shapes=[pltpu.VMEM((LAGS, q * cl, cl), jnp.bfloat16), dma((LAGS,))],
+        compiler_params=pltpu.CompilerParams(vmem_limit_bytes=2 * LAGS * q * cl * cl + (16 << 20)),
+        name="multiply",
+    )(row_t, turned)
 
 
 def solution(mesh):

time: 24.7 us -> 22 us (0.89)
  local copies, waits for them, and re-layouts: 3.29 us -> 0 us
  Pallas kernels: 21.2 us -> 21.9 us
    unnamed x5 -> x0, local copies, waits for them, and re-layouts: 3.29 us -> none
    pallas_call x1 -> x2, Pallas kernels: 21.2 us -> 21.9 us  [the longest x1 19.2 us: correlate(): pl.pallas_call(functools.partial(gather, n, m), out_shape=(pltpu.VMEM((q...]
where the time goes in v2:
time: 22 us; the launch traced here: 21.9 us
  Pallas kernels  21.9 us (100%)
    pallas_call x1, Pallas kernels, correlate(): pl.pallas_call(functools.partial(gather, n, m), out_shape=(pltpu.VMEM((q...  19.2 us
    pallas_call x1, Pallas kernels, correlate(): pl.pallas_call(functools.partial(multiply, scale), out_shape=jax.ShapeDty...  2.65 us

profile of v2, /device:TPU:5, one launch (start us, length us, event | category | flops | bytes accessed | tf_op | source)
XLA Modules:
  0.0 21.9 jit_solution(3656399460244909266)
XLA Ops:
  0.0 19.2 %gather.1 = (bf16[512,512]{1,0:T(8,128)(2,1)S(1)}, bf16[6,512,512]{2,1,0:T(8,128)(2,1)S(1)}) custom-call(bf16[2,2,32,512]{3,2,1,0:T(8,128)(2,1)} %x_hbm.1, f32[32,12]{1,0:T(8,128)} %constant.2.clone.tab_hbm), custom_call_target="tpu_custom_call" | custom-call | tf_op jit(solution)/shard_map/gather/pallas_call | solution.py:239
  19.2 2.6 %multiply.1 = bf16[6,512,512]{2,1,0:T(8,128)(2,1)} custom-call(bf16[512,512]{1,0:T(8,128)(2,1)S(1)} %get-tuple-element.7.row_t, bf16[6,512,512]{2,1,0:T(8,128)(2,1)S(1)} %get-tuple-element.8.turned), custom_call_target="tpu_custom_call" | custom-call | tf_op jit(solution)/shard_map/multiply/pallas_call | solution.py:264

commit v3 on v2

--- a/solution.py
+++ b/solution.py
@@ -43,13 +43,8 @@
     for d in range(1, m):
         pl.semaphore_signal(barrier, inc=1, device_id={"col": (c + d) % m}, device_id_type=MESH)
 
-    @pl.when(r > 0)
-    def _():
-        pl.semaphore_signal(barrier, inc=1, device_id={"row": r - 1}, device_id_type=MESH)
-
-    @pl.when(r < n - 1)
-    def _():
-        pl.semaphore_signal(barrier, inc=1, device_id={"row": r + 1}, device_id_type=MESH)
+    for step in (1, n - 1):
+        pl.semaphore_signal(barrier, inc=1, device_id={"row": (r + step) % n}, device_id_type=MESH)
 
     load_x.wait()
     for w in range(wl):
@@ -60,17 +55,28 @@
         col[r, 0, w * bins:(w + 1) * bins, :] = (re / root).astype(jnp.bfloat16)
         col[r, 1, w * bins:(w + 1) * bins, :] = (im / root).astype(jnp.bfloat16)
 
-    pl.semaphore_wait(barrier, (m - 1) + (r > 0).astype(jnp.int32) + (r < n - 1).astype(jnp.int32))
+    pl.semaphore_wait(barrier, m + 1)
+
+    last = n - 2
+
+    def straight(s):
+        return s == last and n > 2
 
     def z_copy(way, s, part):
-        src = r - s if way == RIGHT else r + s
-        to = r + 1 if way == RIGHT else r - 1
+        if straight(s):
+            src = r
+            to = n - 1 if way == RIGHT else 0
+        else:
+            src = r - s if way == RIGHT else r + s
+            to = r + 1 if way == RIGHT else r - 1
         return pltpu.make_async_remote_copy(
             src_ref=col.at[src, part], dst_ref=col.at[src, part],
             send_sem=z_send.at[way, s, part], recv_sem=z_recv.at[way, s, part],
             device_id={"row": to}, device_id_type=MESH)
 
     def z_sends(way, s):
+        if straight(s):
+            return r == (0 if way == RIGHT else n - 1)
         if way == RIGHT:
             return jnp.logical_and(r - s >= 0, r + 1 < n)
         return jnp.logical_and(r + s < n, r - 1 >= 0)
@@ -155,6 +161,12 @@
                         swap_copy(o, src, slot, part).wait_recv()
                 row_t[chans, pl.ds(base, depth)] = row[o, src].reshape(depth, cl).T
 
+    for way in (LEFT, RIGHT):
+        if straight(last):
+            @pl.when(z_sends(way, last))
+            def _():
+                for part in range(2):
+                    z_copy(way, last, part).start()
     for part in range(2):
         for way in (LEFT, RIGHT):
             @pl.when(z_sends(way, 0))
@@ -179,7 +191,7 @@
                 @pl.when(z_got(way, s))
                 def _():
                     z_copy(way, s, part).wait_recv()
-                    if s + 1 < n - 1:
+                    if s + 1 <= last and not straight(s + 1):
                         @pl.when(z_sends(way, s + 1))
                         def _():
                             z_copy(way, s + 1, part).start()

time: 22 us -> 22.3 us (1.014)
  Pallas kernels: 21.9 us -> 22.2 us
    pallas_call x1, Pallas kernels: 19.2 us -> 19.5 us  [correlate(): pl.pallas_call(functools.partial(gather, n, m), out_shape=(pltpu.VMEM((q...]
where the time goes in v3:
time: 22.3 us; the launch traced here: 22.2 us
  Pallas kernels  22.2 us (100%)
    pallas_call x1, Pallas kernels, correlate(): pl.pallas_call(functools.partial(gather, n, m), out_shape=(pltpu.VMEM((q...  19.5 us
    pallas_call x1, Pallas kernels, correlate(): pl.pallas_call(functools.partial(multiply, scale), out_shape=jax.ShapeDty...  2.65 us

profile of v3, /device:TPU:5, one launch (start us, length us, event | category | flops | bytes accessed | tf_op | source)
XLA Modules:
  0.0 22.2 jit_solution(9557338359740397375)
XLA Ops:
  0.0 19.5 %gather.1 = (bf16[512,512]{1,0:T(8,128)(2,1)S(1)}, bf16[6,512,512]{2,1,0:T(8,128)(2,1)S(1)}) custom-call(bf16[2,2,32,512]{3,2,1,0:T(8,128)(2,1)} %x_hbm.1, f32[32,12]{1,0:T(8,128)} %constant.2.clone.tab_hbm), custom_call_target="tpu_custom_call" | custom-call | tf_op jit(solution)/shard_map/gather/pallas_call | solution.py:251
  19.5 2.6 %multiply.1 = bf16[6,512,512]{2,1,0:T(8,128)(2,1)} custom-call(bf16[512,512]{1,0:T(8,128)(2,1)S(1)} %get-tuple-element.7.row_t, bf16[6,512,512]{2,1,0:T(8,128)(2,1)S(1)} %get-tuple-element.8.turned), custom_call_target="tpu_custom_call" | custom-call | tf_op jit(solution)/shard_map/multiply/pallas_call | solution.py:276
